TPU v7x, 32 devices: a whole 2x2x4 slice. The times are simulated.
32 devices in a mesh: wide: 32 (over z, y, x, core), batch: 1.
Axes of the slice: x: 2, y: 2, z: 4, core: 2. Of those that a mesh axis runs over, the one named last changes fastest.
Arguments:
- q_latent: bfloat16 [1, 64, 4, 1536], P('batch', 'wide'), may hold values from -6 to 6
- draft_start: int32 [1, 64], P('batch', 'wide'), may hold values from 4096 to 8191
- cache_len: int32 [1, 64], P('batch', 'wide'), may hold values from 1 to 4092, 163680 in all within a row
- latent_cache: bfloat16 [1, 64, 4096, 576], P('batch', 'wide'), may hold values from -576 to 576
- w_q_up: bfloat16 [1536, 24576], P('batch', 'wide'), may hold values from -0.15625 to 0.15625
- w_k_absorb: bfloat16 [128, 128, 512], P('wide'), may hold values from -0.5 to 0.5
- value_up_weight: bfloat16 [128, 512, 128], P('wide'), may hold values from -0.25 to 0.25
Outputs:
- values: bfloat16 [1, 64, 4, 16384], P('batch', None, None, 'wide')
All inputs are finite; a program needn't handle non-finite values. No bound on the sum of `cache_len` on one device may be relied on, other than what follows from the above.
Results may differ from a plain program's by a relative error of at most 0.014.
The roundings to bfloat16 on the way count: a program that leaves them out, or rounds other values in their place, can miss the bound.
Values may be sent and summed in bfloat16 or wider, within the bound.
A program may use at most 128 MiB of HBM per device.

v0:
```python
import jax
import jax.numpy as jnp
from jax import lax
from jax.sharding import PartitionSpec as P


def turn_rotary(query_rope, positions, rope_width):
    half_width = rope_width // 2
    freqs = 10000.0 ** (-jnp.arange(half_width).astype(jnp.float32) * 2.0 / rope_width)
    angles = positions.astype(jnp.float32)[:, :, None, None] * freqs
    cosine = jnp.cos(angles)
    sine_table = jnp.sin(angles)
    first_half = query_rope[..., :half_width]
    second_half = query_rope[..., half_width:]
    return jnp.concatenate(
        [
            first_half * cosine - second_half * sine_table,
            second_half * cosine + first_half * sine_table,
        ],
        axis=-1,
    )


def attend_request(query_matrix, cache, length, drafts, kv_width, scale):
    context_rows = cache.shape[0]
    row_count = query_matrix.shape[0]
    scores = lax.dot_general(
        query_matrix, cache, (((1,), (1,)), ((), ())), preferred_element_type=jnp.float32
    )
    scores = scores.reshape(drafts, row_count // drafts, context_rows) * scale
    slots = lax.iota(jnp.int32, context_rows)
    limit = length + lax.iota(jnp.int32, drafts)
    visible = slots[None, None, :] <= limit[:, None, None]
    peak = jnp.max(jnp.where(visible, scores, -jnp.inf), axis=2, keepdims=True)
    expo = jnp.where(visible, jnp.exp(scores - peak), 0.0)
    probs = (
        (expo / jnp.sum(expo, axis=2, keepdims=True))
        .astype(jnp.bfloat16)
        .reshape(row_count, context_rows)
    )
    latent_output = jnp.dot(probs, cache[:, :kv_width], preferred_element_type=jnp.float32)
    return latent_output.astype(jnp.bfloat16)


def per_device(q_latent, draft_start, cache_len, latent_cache, w_q_up, w_k_absorb, value_up_weight):
    heads_here = w_k_absorb.shape[0]
    nope_width = w_k_absorb.shape[1]
    kv_width = w_k_absorb.shape[2]
    head_dim = w_q_up.shape[1] // heads_here
    rope_width = head_dim - nope_width
    scale = float(head_dim) ** (-0.5)
    gathered, start_all = (
        lax.all_gather(q_latent, "wide", axis=1, tiled=True),
        lax.all_gather(draft_start, "wide", axis=1, tiled=True),
    )
    group_requests = gathered.shape[1]
    drafts = gathered.shape[2]
    flat_rows = gathered.reshape(group_requests * drafts, gathered.shape[3])
    q_full = jnp.dot(
        flat_rows,
        lax.all_gather(w_q_up, "batch", axis=0, tiled=True),
        preferred_element_type=jnp.float32,
    )
    q_full = q_full.astype(jnp.bfloat16).reshape(group_requests, drafts, heads_here, head_dim)
    query_nope = q_full[..., :nope_width]
    query_rope = q_full[..., nope_width:].astype(jnp.float32)
    absorbed = jnp.einsum(
        "rdhn,hnk->rdhk", query_nope, w_k_absorb, preferred_element_type=jnp.float32
    )
    positions = start_all[0][:, None] + lax.iota(jnp.int32, drafts)[None, :]
    rotated_rows = turn_rotary(query_rope, positions, rope_width)
    query = jnp.concatenate([absorbed, rotated_rows], axis=-1).astype(jnp.bfloat16)
    query = query.reshape(group_requests, drafts, 1, heads_here, kv_width + rope_width)
    arrived = lax.all_to_all(query, "wide", split_axis=0, concat_axis=2, tiled=True)
    owned = arrived.shape[0]
    senders = arrived.shape[2]
    items = arrived.shape[3]
    results = []
    for which in range(owned):
        query_matrix = arrived[which].reshape(drafts * senders * items, arrived.shape[4])
        out_rows = attend_request(
            query_matrix, latent_cache[0, which], cache_len[0, which], drafts, kv_width, scale
        )
        results.append(out_rows.reshape(drafts, senders, items, kv_width))
    stacked = jnp.stack(results, axis=0)
    latent_output = lax.all_to_all(stacked, "wide", split_axis=2, concat_axis=0, tiled=True)
    latent_output = latent_output.reshape(group_requests, drafts, heads_here, kv_width)
    values = jnp.einsum(
        "aofu,fub->aofb", latent_output, value_up_weight, preferred_element_type=jnp.float32
    )
    return values.astype(jnp.bfloat16).reshape(
        1, group_requests, drafts, heads_here * value_up_weight.shape[2]
    )


def solution(mesh):
    in_specs = (
        P("batch", "wide", None, None),
        P("batch", "wide"),
        P("batch", "wide"),
        P("batch", "wide", None, None),
        P("batch", "wide"),
        P("wide", None, None),
        P("wide", None, None),
    )
    out_specs = P("batch", None, None, "wide")
    return jax.shard_map(
        per_device, mesh=mesh, in_specs=in_specs, out_specs=out_specs, check_vma=False
    )
```

profile of v0, /device:TPU:1, one launch (start us, length us, event | category | flops | bytes accessed | tf_op | source)
XLA Modules:
  0.0 202.4 jit_solution(11057095233757509568)
XLA Ops:
  0.0 45.6 %all_gather.7 = bf16[1,64,4,1536]{3,2,0,1:T(4,128)(2,1)S(1)} all-gather(bf16[1,2,4,1536]{3,2,0,1:T(4,128)(2,1)} %bitcast.69), channel_id=1, replica_groups=mesh['wide'=32,'batch'=1] {'wide'}, dimensions={1}, use_global_device_ids=true | all-gather | bytes 811008 | tf_op jit(solution)/shard_map/all_gather | solution.py:53
  45.6 1.1 reshape.173
  46.7 2.0 convolution_convert_fusion.1
  48.7 0.5 reshape.174
  49.5 35.5 %all-reduce = s32[64]{0:T(128)S(1)} all-reduce(s32[64]{0:T(128)S(1)} %bitcast_dynamic-update-slice_fusion), channel_id=1, replica_groups=mesh['wide'=32,'batch'=1] {'wide'}, use_global_device_ids=true, to_apply=%add | all-reduce | flops 64 | bytes 512
  85.1 0.5 multiply_cosine_fusion
  85.7 0.4 fusion.26
  86.1 0.3 fusion.39
  86.4 0.2 pad_maximum_fusion
  86.6 2.1 %copy.24 = bf16[64,4,1,4,576]{4,1,3,2,0:T(4,128)(2,1)} copy(bf16[64,4,1,4,576]{4,0,1,3,2:T(8,128)(2,1)S(1)} %pad_maximum_fusion) | data formatting | bytes 2359296 | tf_op jit(solution)/shard_map/concatenate | solution.py:72
  88.7 6.3 %all-to-all-start = ((bf16[64,4,1,4,576]{4,1,3,2,0:T(4,128)(2,1)}), bf16[64,4,1,4,576]{4,1,3,2,0:T(4,128)(2,1)S(1)}, u32[]{:S(2)}, u32[]{:S(2)}) async-start(bf16[64,4,1,4,576]{4,1,3,2,0:T(4,128)(2,1)} %copy.24), calls=%async_computation | async-start | bytes 2621440 | tf_op jit(solution)/shard_map/all_to_all | solution.py:74
  95.0 0.6 fusion.47
  95.6 0.6 iota_add_fusion
  96.2 0.7 iota_add_fusion.1
  97.0 8.7 %slice_bitcast_fusion.1 = (bf16[4096,576]{0,1:T(8,128)(2,1)}, bf16[4096,576]{0,1:T(8,128)(2,1)}) fusion(bf16[1,2,4096,576]{2,3,1,0:T(8,128)(2,1)} %param.10), kind=kLoop, calls=%fused_computation.29 | loop fusion | bytes 18874368 | tf_op jit(solution)/shard_map/squeeze | solution.py:82
  105.7 20.5 %all-to-all-done = bf16[64,4,1,4,576]{4,1,3,2,0:T(4,128)(2,1)S(1)} async-done(((bf16[64,4,1,4,576]{4,1,3,2,0:T(4,128)(2,1)}), bf16[64,4,1,4,576]{4,1,3,2,0:T(4,128)(2,1)S(1)}, u32[]{:S(2)}, u32[]{:S(2)}) %all-to-all-start) | async-done | bytes 1179680 | tf_op jit(solution)/shard_map/all_to_all | solution.py:74
  126.2 0.5 copy.51
  126.7 0.5 fusion.46
  127.2 8.2 %fusion.10 = f32[4,128,4096]{2,1,0:T(8,128)} fusion(bf16[1,2,4096,576]{2,3,1,0:T(8,128)(2,1)} %param.10, bf16[4,128,576]{2,0,1:T(4,128)(2,1)S(1)} %bitcast.68), kind=kOutput, calls=%fused_computation.12 | convolution fusion | flops 2415919104 | bytes 13697024 | tf_op jit(solution)/shard_map/dot_general | solution.py:27
  135.4 5.7 %fusion.12 = f32[4,128,4096]{2,1,0:T(8,128)} fusion(bf16[1,2,4096,576]{2,3,1,0:T(8,128)(2,1)S(1)} %bitcast.57, bf16[4,128,576]{2,0,1:T(4,128)(2,1)S(1)} %bitcast.67), kind=kOutput, calls=%fused_computation.14 | convolution fusion | flops 2415919104 | bytes 13762560 | tf_op jit(solution)/shard_map/dot_general | solution.py:27
  141.1 8.9 %fusion.49 = (f32[4,128]{1,0:T(4,128)S(1)}, f32[4,128,4096]{2,1,0:T(8,128)S(1)}) fusion(f32[4,128,4096]{2,1,0:T(8,128)} %fusion.12, pred[4,4096]{1,0:T(4,128)(4,1)S(1)} %iota_compare_fusion.1), kind=kOutput, calls=%fused_computation.67 | output fusion | flops 12587007 | bytes 16795648 | tf_op jit(solution)/shard_map/sub | solution.py:35
  150.0 1.4 divide_convert_fusion.1
  151.4 2.4 %fusion.27 = bf16[512,512]{1,0:T(8,128)(2,1)S(1)} fusion(bf16[512,4096]{1,0:T(8,128)(2,1)S(1)} %bitcast.65, bf16[4096,576]{0,1:T(8,128)(2,1)S(1)} %bitcast.63), kind=kOutput, calls=%fused_computation.34 | convolution fusion | flops 2147745792 | bytes 8912896 | tf_op jit(solution)/shard_map/dot_general | solution.py:41
  154.0 9.0 %fusion.48 = (f32[4,128]{1,0:T(4,128)S(1)}, f32[4,128,4096]{2,1,0:T(8,128)S(1)}) fusion(f32[4,128,4096]{2,1,0:T(8,128)} %fusion.10, pred[4,4096]{1,0:T(4,128)(4,1)S(1)} %iota_compare_fusion), kind=kOutput, calls=%fused_computation.66 | output fusion | flops 12587007 | bytes 16795648 | tf_op jit(solution)/shard_map/sub | solution.py:35
  163.0 1.4 divide_convert_fusion
  164.4 3.4 %fusion.30 = bf16[512,512]{1,0:T(8,128)(2,1)} fusion(bf16[512,4096]{1,0:T(8,128)(2,1)S(1)} %bitcast.64, bf16[4096,576]{0,1:T(8,128)(2,1)S(1)} %bitcast.61), kind=kOutput, calls=%fused_computation.35 | convolution fusion | flops 2147745792 | bytes 8912896 | tf_op jit(solution)/shard_map/dot_general | solution.py:41
  167.8 1.3 stack_reshape.7
  169.1 0.7 pad_maximum_fusion.1
  169.9 0.6 copy.35
  170.5 29.6 %all_to_all.30 = bf16[2,4,32,4,512]{4,3,1,0,2:T(4,128)(2,1)S(1)} all-to-all(bf16[2,4,32,4,512]{4,3,1,0,2:T(4,128)(2,1)S(1)} %copy.35), channel_id=1, replica_groups=mesh['wide'=32,'batch'=1] {'wide'}, dimensions={2} | all-to-all | bytes 2097152 | tf_op jit(solution)/shard_map/all_to_all | solution.py:86
  200.1 1.3 fusion.33
  201.6 0.8 reshape.186
  (40 shorter events, 0.9 us)
Async XLA Ops:
  0.0 46.7 %copy-start = (bf16[1536,768]{1,0:T(8,128)(2,1)S(1)}, bf16[1536,768]{1,0:T(8,128)(2,1)}, u32[]{:S(2)}) copy-start(bf16[1536,768]{1,0:T(8,128)(2,1)} %param.11) | copy-start | bytes 7077892
  0.0 49.4 %copy-start.5 = (s32[1,2]{1,0:T(1,128)S(1)}, s32[1,2]{1,0:T(1,128)}, u32[]{:S(2)}) copy-start(s32[1,2]{1,0:T(1,128)} %param.8) | copy-start | bytes 28
  46.7 38.9 %copy-start.2 = (bf16[4,128,512]{2,1,0:T(8,128)(2,1)S(1)}, bf16[4,128,512]{2,1,0:T(8,128)(2,1)}, u32[]{:S(2)}) copy-start(bf16[4,128,512]{2,1,0:T(8,128)(2,1)} %param.12) | copy-start | bytes 1572868
  86.1 8.9 %copy-start.3 = (s32[1,2]{1,0:T(1,128)S(1)}, s32[1,2]{1,0:T(1,128)}, u32[]{:S(2)}) copy-start(s32[1,2]{1,0:T(1,128)} %param.9) | copy-start | bytes 28
  88.7 37.5 %all-to-all-start = ((bf16[64,4,1,4,576]{4,1,3,2,0:T(4,128)(2,1)}), bf16[64,4,1,4,576]{4,1,3,2,0:T(4,128)(2,1)S(1)}, u32[]{:S(2)}, u32[]{:S(2)}) async-start(bf16[64,4,1,4,576]{4,1,3,2,0:T(4,128)(2,1)} %copy.24), calls=%async_computation | async-start | bytes 2621440 | tf_op jit(solution)/shard_map/all_to_all | solution.py:74
  126.7 8.7 %slice-start = ((s8[9437184]{0:T(1024)(128)(4,1)}), s8[4194304]{0:T(1024)(128)(4,1)S(1)}, s32[]{:S(2)}) async-start(s8[9437184]{0:T(1024)(128)(4,1)} %bitcast.56), calls=%async_computation.2 | async-start | bytes 8388608
  127.1 8.3 %slice-start.1 = ((s8[9437184]{0:T(1024)(128)(4,1)}), s8[4194304]{0:T(1024)(128)(4,1)S(1)}, s32[]{:S(2)}) async-start(s8[9437184]{0:T(1024)(128)(4,1)} %bitcast.56), calls=%async_computation.3 | async-start | bytes 8388608
  127.2 8.3 %slice-start.2 = ((s8[9437184]{0:T(1024)(128)(4,1)}), s8[1048576]{0:T(1024)(128)(4,1)S(1)}, s32[]{:S(2)}) async-start(s8[9437184]{0:T(1024)(128)(4,1)} %bitcast.56), calls=%async_computation.4 | async-start | bytes 2097152
  135.4 16.0 %slice-start.5 = ((s8[4718592]{0:T(1024)(128)(4,1)}), s8[4194304]{0:T(1024)(128)(4,1)S(1)}, s32[]{:S(2)}) async-start(s8[4718592]{0:T(1024)(128)(4,1)} %bitcast.62), calls=%async_computation.7 | async-start | bytes 8388608
  141.1 10.3 %slice-start.6 = ((s8[4718592]{0:T(1024)(128)(4,1)}), s8[524288]{0:T(1024)(128)(4,1)S(1)}, s32[]{:S(2)}) async-start(s8[4718592]{0:T(1024)(128)(4,1)} %bitcast.62), calls=%async_computation.8 | async-start | bytes 1048576
  151.4 12.9 %slice-start.3 = ((s8[4718592]{0:T(1024)(128)(4,1)}), s8[524288]{0:T(1024)(128)(4,1)S(1)}, s32[]{:S(2)}) async-start(s8[4718592]{0:T(1024)(128)(4,1)} %bitcast.60), calls=%async_computation.5 | async-start | bytes 1048576
  153.9 10.4 %slice-start.4 = ((s8[4718592]{0:T(1024)(128)(4,1)}), s8[4194304]{0:T(1024)(128)(4,1)S(1)}, s32[]{:S(2)}) async-start(s8[4718592]{0:T(1024)(128)(4,1)} %bitcast.60), calls=%async_computation.6 | async-start | bytes 8388608
  167.8 34.6 %copy-start.1 = (bf16[1536,768]{1,0:T(8,128)(2,1)S(1)}, bf16[1536,768]{1,0:T(8,128)(2,1)}, u32[]{:S(2)}) copy-start(bf16[1536,768]{1,0:T(8,128)(2,1)} %param.11) | copy-start | bytes 7077892
  169.1 31.0 %copy-start.4 = (bf16[4,512,128]{2,1,0:T(8,128)(2,1)S(1)}, bf16[4,512,128]{2,1,0:T(8,128)(2,1)}, u32[]{:S(2)}) copy-start(bf16[4,512,128]{2,1,0:T(8,128)(2,1)} %param.13) | copy-start | bytes 1572868
where the time goes:
time: 204 us; the launch traced here: 202 us
  blocking collectives  111 us (54%)
  other arithmetic  23.9 us (12%)
  matrix products  23.3 us (11%)
  waiting for transfers between devices  20.5 us (10%)
  local copies, waits for them, and re-layouts  17.2 us (8%)
  starting transfers between devices  6.26 us (3%)
    all_gather x1, blocking collectives, per_device(): lax.all_gather(q_latent, 'wide', axis=1, tiled=True)  45.6 us
    unnamed x1, blocking collectives  35.5 us
    all_to_all x1, blocking collectives, per_device(): lax.all_to_all(stacked, 'wide', split_axis=2, concat_axis=0, tiled=True)  29.6 us
    all_to_all x1, waiting for transfers between devices, per_device(): lax.all_to_all(query, 'wide', split_axis=0, concat_axis=2, tiled=True)  20.5 us
    sub x2, other arithmetic, attend_request(): expo = jnp.where(visible, jnp.exp(scores - peak), 0.0)  17.9 us
    dot_general x2, matrix products, attend_request(): lax.dot_general(query_matrix, cache, (((1,), (1,)), ((), ())), preferred_...  13.9 us
    squeeze x1, local copies, waits for them, and re-layouts, per_device(): latent_cache[0, which]  8.74 us
    all_to_all x1, starting transfers between devices, per_device(): lax.all_to_all(query, 'wide', split_axis=0, concat_axis=2, tiled=True)  6.26 us
  transfers between devices with their start and end apart: 1, of which 1 were waited for; matrix products, arithmetic and copies ran while one was open for 5% of the time, Pallas kernels for 0%

commit v1 on v0

v1 whole, which is shorter than its diff:
```python
import functools
import math
import jax
import jax.numpy as jnp
from jax import lax
from jax.experimental import pallas as pl
from jax.experimental.pallas import tpu as pltpu
from jax.sharding import PartitionSpec as P

MESH = pl.DeviceIdType.MESH


def spread_step(count):
    step = max(1, int(count * 0.41))
    while math.gcd(step, count) != 1:
        step += 1
    return step


def rotary_tables(draft_start, drafts, heads_here, rope_width):
    half = rope_width // 2
    freqs = 10000.0 ** (-jnp.arange(half).astype(jnp.float32) * 2.0 / rope_width)
    positions = draft_start[None, :] + lax.iota(jnp.int32, drafts)[:, None]
    angles = positions.astype(jnp.float32)[:, :, None] * freqs
    cosine, sine = jnp.cos(angles), jnp.sin(angles)
    owned = draft_start.shape[0]

    def spread(low, high):
        both = jnp.concatenate([low, high], axis=-1).reshape(drafts, 1, owned * rope_width)
        both = jnp.broadcast_to(both, (drafts, heads_here, owned * rope_width))
        return both.reshape(drafts * heads_here, owned * rope_width)

    return spread(cosine, cosine), spread(-sine, sine)


def attend(which, length, query, cache, scores, peak_part, sum_part, acc, drafts, group, kv, coef, chunk):
    rows = query.shape[0]
    ctx = cache.shape[1]
    lanes = peak_part.shape[1]
    row = lax.broadcasted_iota(jnp.int32, (rows, 1), 0)
    limit = length + lax.rem(row, group) // (group // drafts)
    peak_part[...] = jnp.full_like(peak_part, -jnp.inf)
    sum_part[...] = jnp.zeros_like(sum_part)
    acc[...] = jnp.zeros_like(acc)

    def fold(part, op):
        out = part[:, :lanes]
        for at in range(lanes, chunk, lanes):
            out = op(out, part[:, at:at + lanes])
        return out

    def score(step, carry):
        base = pl.multiple_of(step * chunk, chunk)
        part = lax.dot_general(
            query[...], cache[which, pl.ds(base, chunk), :], (((1,), (1,)), ((), ())),
            preferred_element_type=jnp.float32,
        )
        slot = base + lax.broadcasted_iota(jnp.int32, (1, chunk), 1)
        part = jnp.where(slot <= limit, part, -jnp.inf)
        scores[:, pl.ds(base, chunk)] = part
        peak_part[...] = jnp.maximum(peak_part[...], fold(part, jnp.maximum))
        return carry

    lax.fori_loop(0, ctx // chunk, score, 0)
    peak = jnp.max(peak_part[...], axis=1, keepdims=True) * coef

    def expo(step, carry):
        base = pl.multiple_of(step * chunk, chunk)
        part = jnp.exp2(scores[:, pl.ds(base, chunk)] * coef - peak)
        scores[:, pl.ds(base, chunk)] = part
        sum_part[...] += fold(part, jnp.add)
        return carry

    lax.fori_loop(0, ctx // chunk, expo, 0)
    inverse = 1.0 / jnp.sum(sum_part[...], axis=1, keepdims=True)

    def weigh(step, carry):
        base = pl.multiple_of(step * chunk, chunk)
        probs = (scores[:, pl.ds(base, chunk)] * inverse).astype(jnp.bfloat16)
        acc[...] += jnp.dot(
            probs, cache[which, pl.ds(base, chunk), :kv], preferred_element_type=jnp.float32
        )
        return carry

    lax.fori_loop(0, ctx // chunk, weigh, 0)


def kernel(
    n, drafts, heads_here, nope, rope, kv, vd, coef, chunk,
    length_ref, latent_ref, cos_ref, sin_ref, cache_hbm, wq_hbm, wk_hbm, wv_hbm,
    out_ref,
    cache, wq, wk, wv, q_full, wide_f32, rope_f32, send_q, send_r, recv_q, recv_r,
    query, scores, peak_part, sum_part, acc, send_o, recv_o,
    cache_sem, wq_sem, wk_sem, wv_sem, own_sem,
    sq_sem, sr_sem, so_sem, rq_sem, rr_sem, ro_sem,
):
    me = lax.axis_index("wide")
    owned = cache.shape[0]
    group = drafts * heads_here
    head_dim = nope + rope
    step = spread_step(n)

    def partner(t):
        return lax.rem(me + lax.rem(t * step, n), n)

    load_q = pltpu.make_async_copy(wq_hbm, wq, wq_sem)
    load_k = pltpu.make_async_copy(wk_hbm, wk, wk_sem)
    load_v = pltpu.make_async_copy(wv_hbm, wv, wv_sem)
    loads = [
        pltpu.make_async_copy(cache_hbm.at[which], cache.at[which], cache_sem.at[which])
        for which in range(owned)
    ]
    load_q.start()
    load_k.start()
    for load in loads:
        load.start()
    load_v.start()

    barrier = pltpu.get_barrier_semaphore()

    def greet(t, carry):
        pl.semaphore_signal(barrier, inc=1, device_id={"wide": partner(t)}, device_id_type=MESH)
        return carry

    lax.fori_loop(1, n, greet, 0)

    load_q.wait()
    columns = heads_here * head_dim
    block = 256 if columns % 256 == 0 else columns
    for at in range(0, columns, block):
        part = jnp.dot(latent_ref[...], wq[:, at:at + block], preferred_element_type=jnp.float32)
        q_full[:, at:at + block] = part.astype(jnp.bfloat16).astype(jnp.float32)
    load_k.wait()
    rows = q_full.shape[0]
    for head in range(heads_here):
        at = head * head_dim
        absorbed = jnp.dot(
            q_full[:, at:at + nope].astype(jnp.bfloat16), wk[head],
            preferred_element_type=jnp.float32,
        )
        for part in range(kv // 128):
            wide_f32[part, pl.ds(head, rows, stride=heads_here), :] = absorbed[:, part * 128:part * 128 + 128]
        tail = q_full[:, at + nope:at + head_dim]
        rope_f32[pl.ds(head, rows, stride=heads_here), :] = jnp.concatenate([tail] * owned, axis=-1)
    for part in range(kv // 128):
        packed = wide_f32[part].astype(jnp.bfloat16).reshape(n, owned, group, 128)
        for which in range(owned):
            send_q[which, :, :, part * 128:part * 128 + 128] = packed[:, which]
    turned = rope_f32[:, :rope].reshape(n, owned, group, rope)
    send_r[...] = jnp.concatenate(
        [turned[:, which] for which in range(owned)], axis=-1
    ).astype(jnp.bfloat16)

    pl.semaphore_wait(barrier, n - 1)

    def post(t, carry, which):
        d = partner(t)
        if which == 0:
            pltpu.make_async_remote_copy(
                src_ref=send_r.at[d], dst_ref=recv_r.at[me], send_sem=sr_sem, recv_sem=rr_sem,
                device_id={"wide": d}, device_id_type=MESH,
            ).start()
        pltpu.make_async_remote_copy(
            src_ref=send_q.at[which, d], dst_ref=recv_q.at[which, me],
            send_sem=sq_sem.at[which], recv_sem=rq_sem.at[which],
            device_id={"wide": d}, device_id_type=MESH,
        ).start()
        return carry

    for which in range(owned):
        lax.fori_loop(1, n, functools.partial(post, which=which), 0)
        own = pltpu.make_async_copy(send_q.at[which, me], recv_q.at[which, me], own_sem)
        own.start()
        own.wait()
    own = pltpu.make_async_copy(send_r.at[me], recv_r.at[me], own_sem)
    own.start()
    own.wait()

    def all_but_one(ref, sem):
        pltpu.make_async_copy(ref.at[pl.ds(0, n - 1)], ref.at[pl.ds(0, n - 1)], sem).wait()

    def post_out(t, carry, which):
        d = partner(t)
        pltpu.make_async_remote_copy(
            src_ref=send_o.at[which, d], dst_ref=recv_o.at[which, me],
            send_sem=so_sem.at[which], recv_sem=ro_sem.at[which],
            device_id={"wide": d}, device_id_type=MESH,
        ).start()
        return carry

    all_but_one(recv_r, rr_sem)
    turn = recv_r[...].astype(jnp.float32)
    width = turn.shape[2]
    flat = turn.reshape(n * group, width)
    lane = lax.broadcasted_iota(jnp.int32, (1, width), 1)
    half = rope // 2
    swapped = jnp.where(
        lax.rem(lane, rope) < half,
        pltpu.roll(flat, width - half, 1),
        pltpu.roll(flat, half, 1),
    ).reshape(n, group, width)
    rotated = (turn * cos_ref[...][None] + swapped * sin_ref[...][None]).reshape(n * group, width)
    rope_f32[:n * group, :] = rotated

    for which in range(owned):
        all_but_one(recv_q.at[which], rq_sem.at[which])
        query[:, :kv] = recv_q[which].reshape(n * group, kv)
        query[:, kv:] = rope_f32[:n * group, which * rope:(which + 1) * rope].astype(jnp.bfloat16)
        loads[which].wait()
        attend(
            which, length_ref[which], query, cache, scores, peak_part, sum_part, acc,
            drafts, group, kv, coef, chunk,
        )
        send_o[which] = acc[...].astype(jnp.bfloat16).reshape(n, group, kv)
        lax.fori_loop(1, n, functools.partial(post_out, which=which), 0)
        own = pltpu.make_async_copy(send_o.at[which, me], recv_o.at[which, me], own_sem)
        own.start()
        own.wait()

    load_v.wait()
    for which in range(owned):
        all_but_one(recv_o.at[which], ro_sem.at[which])
    for part in range(kv // 128):
        lanes = slice(part * 128, part * 128 + 128)
        arrived = jnp.stack([recv_o[which, :, :, lanes] for which in range(owned)], axis=1)
        wide_f32[part] = arrived.astype(jnp.float32).reshape(n * owned * group, 128)
    for head in range(heads_here):
        mine = jnp.concatenate(
            [wide_f32[part, pl.ds(head, rows, stride=heads_here), :] for part in range(kv // 128)], axis=-1
        ).astype(jnp.bfloat16)
        out_ref[:, head * vd:(head + 1) * vd] = jnp.dot(
            mine, wv[head], preferred_element_type=jnp.float32
        ).astype(jnp.bfloat16)

    all_but_one(send_r, sr_sem)
    for which in range(owned):
        all_but_one(send_q.at[which], sq_sem.at[which])
        all_but_one(send_o.at[which], so_sem.at[which])


def per_device(q_latent, draft_start, cache_len, latent_cache, w_q_up, w_k_absorb, value_up_weight):
    n = lax.axis_size("wide")
    heads_here, nope, kv = w_k_absorb.shape
    vd = value_up_weight.shape[2]
    head_dim = w_q_up.shape[1] // heads_here
    rope = head_dim - nope
    owned, ctx, width = latent_cache.shape[1:]
    drafts, ql = q_latent.shape[2:]
    group = drafts * heads_here
    rows = n * owned * drafts
    chunk = min(512, ctx)
    coef = float(head_dim) ** -0.5 * math.log2(math.e)
    bf16, f32 = jnp.bfloat16, jnp.float32

    latent = lax.all_gather(q_latent[0], "wide", axis=0, tiled=True).reshape(rows, ql)
    wq = lax.all_gather(w_q_up, "batch", axis=0, tiled=True)
    cosine, sine = rotary_tables(draft_start[0], drafts, heads_here, rope)

    vmem = pl.BlockSpec(memory_space=pltpu.VMEM)
    hbm = pl.BlockSpec(memory_space=pl.ANY)
    dma = pltpu.SemaphoreType.DMA
    out = pl.pallas_call(
        functools.partial(kernel, n, drafts, heads_here, nope, rope, kv, vd, coef, chunk),
        out_shape=jax.ShapeDtypeStruct((rows, heads_here * vd), bf16),
        in_specs=[pl.BlockSpec(memory_space=pltpu.SMEM), vmem, vmem, vmem, hbm, hbm, hbm, hbm],
        out_specs=vmem,
        scratch_shapes=[
            pltpu.VMEM((owned, ctx, width), bf16),
            pltpu.VMEM(wq.shape, bf16),
            pltpu.VMEM(w_k_absorb.shape, bf16),
            pltpu.VMEM(value_up_weight.shape, bf16),
            pltpu.VMEM((rows, heads_here * head_dim), f32),
            pltpu.VMEM((kv // 128, rows * heads_here, 128), f32),
            pltpu.VMEM((rows * heads_here, owned * rope), f32),
            pltpu.VMEM((owned, n, group, kv), bf16),
            pltpu.VMEM((n, group, owned * rope), bf16),
            pltpu.VMEM((owned, n, group, kv), bf16),
            pltpu.VMEM((n, group, owned * rope), bf16),
            pltpu.VMEM((n * group, width), bf16),
            pltpu.VMEM((n * group, ctx), f32),
            pltpu.VMEM((n * group, min(128, chunk)), f32),
            pltpu.VMEM((n * group, min(128, chunk)), f32),
            pltpu.VMEM((n * group, kv), f32),
            pltpu.VMEM((owned, n, group, kv), bf16),
            pltpu.VMEM((owned, n, group, kv), bf16),
            dma((owned,)), dma, dma, dma, dma,
            dma((owned,)), dma, dma((owned,)), dma((owned,)), dma, dma((owned,)),
        ],
        compiler_params=pltpu.CompilerParams(
            collective_id=0, has_side_effects=True, vmem_limit_bytes=56 << 20
        ),
    )(cache_len[0], latent, cosine, sine, latent_cache[0], wq, w_k_absorb, value_up_weight)
    return out.reshape(1, n * owned, drafts, heads_here * vd)


def solution(mesh):
    in_specs = (
        P("batch", "wide", None, None),
        P("batch", "wide"),
        P("batch", "wide"),
        P("batch", "wide", None, None),
        P("batch", "wide"),
        P("wide", None, None),
        P("wide", None, None),
    )
    out_specs = P("batch", None, None, "wide")
    return jax.shard_map(
        per_device, mesh=mesh, in_specs=in_specs, out_specs=out_specs, check_vma=False
    )
```

time: 204 us -> 127 us (0.62)
  the two profiles are of different devices: /device:TPU:1 before, /device:TPU:0 now
where the time goes in v1:
time: 127 us; the launch traced here: 126 us
  Pallas kernels  61.9 us (49%)
  blocking collectives  45.6 us (36%)
  local copies, waits for them, and re-layouts  17.8 us (14%)
    pallas_call x1, Pallas kernels, per_device(): pl.pallas_call(functools.partial(kernel, n, drafts, heads_here, nope, rop...  61.9 us
    all_gather x1, blocking collectives, per_device(): lax.all_gather(q_latent[0], 'wide', axis=0, tiled=True).reshape(rows, ql)  45.6 us
    unnamed x1, local copies, waits for them, and re-layouts  13.6 us

profile of v1, /device:TPU:0, one launch (start us, length us, event | category | flops | bytes accessed | tf_op | source)
XLA Modules:
  0.0 126.2 jit_solution(16882729241968683506)
XLA Ops:
  0.0 0.7 add_convert_fusion
  0.7 0.1 fusion
  0.8 0.1 pad_maximum_fusion
  0.9 0.1 broadcast_in_dim.8
  1.0 0.1 broadcast_in_dim.19
  1.1 0.6 broadcast_in_dim.20
  1.7 0.6 broadcast_in_dim.18
  2.3 45.6 %all-gather = bf16[1,64,4,1536]{3,2,0,1:T(4,128)(2,1)S(1)} all-gather(bf16[1,2,4,1536]{3,2,0,1:T(4,128)(2,1)} %bitcast.11), channel_id=2, replica_groups=mesh['wide'=32,'batch'=1] {'wide'}, dimensions={1}, use_global_device_ids=true | all-gather | bytes 811008 | tf_op jit(solution)/shard_map/all_gather | solution.py:255
  47.9 1.1 reshape.44.latent_ref
  48.9 13.6 %copy.10 = bf16[1,2,4096,576]{3,2,1,0:T(8,128)(2,1)} copy(bf16[1,2,4096,576]{2,3,1,0:T(8,128)(2,1)} %param.10) | data formatting | bytes 18874368 | tf_op args[3]
  62.5 61.9 %shard_map.73 = bf16[256,512]{1,0:T(8,128)(2,1)} custom-call(s32[2]{0:T(128)} %bitcast.12, bf16[256,1536]{1,0:T(8,128)(2,1)} %reshape.44.latent_ref, f32[16,128]{1,0:T(8,128)} %bitcast.10, f32[16,128]{1,0:T(8,128)} %bitcast.9, bf16[2,4096,576]{2,1,0:T(8,128)(2,1)} %bitcast.8, bf16[1536,768]{1,0:T(8,128)(2,1)} %wq_hbm, bf16[4,128,512]{2,1,0:T(8,128)(2,1)} %wk_hbm.1, ...), custom_call_target="tpu_custom_call" | custom-call | tf_op jit(solution)/shard_map/pallas_call | solution.py:262
  124.4 1.7 %reshape.47 = bf16[1,64,4,512]{3,2,1,0:T(4,128)(2,1)} reshape(bf16[256,512]{1,0:T(8,128)(2,1)} %shard_map.73) | data formatting | bytes 524288 | tf_op jit(solution)/shard_map/reshape | solution.py:293
  (1 shorter events, 0.0 us)

commit v2 on v1

v2 whole, which is shorter than its diff:
```python
import functools
import math
import jax
import jax.numpy as jnp
from jax import lax
from jax.experimental import pallas as pl
from jax.experimental.pallas import tpu as pltpu
from jax.sharding import PartitionSpec as P

MESH = pl.DeviceIdType.MESH


def spread_step(count):
    step = max(1, int(count * 0.41))
    while math.gcd(step, count) != 1:
        step += 1
    return step


def rotary_tables(start_ref, freq, drafts, group, rope_width, owned):
    shape = (group, owned * rope_width)
    row = lax.broadcasted_iota(jnp.int32, shape, 0) // (group // drafts)
    lane = lax.broadcasted_iota(jnp.int32, shape, 1)
    start = jnp.full(shape, start_ref[0], jnp.int32)
    for which in range(1, owned):
        start = jnp.where(lane // rope_width == which, start_ref[which], start)
    angle = (start + row).astype(jnp.float32) * freq
    turns = jnp.floor(angle * (0.5 / math.pi) + 0.5)
    angle = angle - turns * 6.28125
    angle = angle - turns * 0.0019340515136718750
    angle = angle - turns * 1.2556659146475769e-06
    sine = jnp.sin(angle)
    sine = jnp.where(lax.rem(lane, rope_width) < rope_width // 2, -sine, sine)
    return jnp.cos(angle), sine


def attend(which, length, query, cache, scores, peak_part, sum_part, acc, drafts, group, kv, coef, chunk):
    rows = query.shape[0]
    ctx = cache.shape[2]
    lanes = peak_part.shape[1]
    row = lax.broadcasted_iota(jnp.int32, (rows, 1), 0)
    limit = length + lax.rem(row, group) // (group // drafts)
    peak_part[...] = jnp.full_like(peak_part, -jnp.inf)
    sum_part[...] = jnp.zeros_like(sum_part)
    acc[...] = jnp.zeros_like(acc)

    def fold(part, op):
        out = part[:, :lanes]
        for at in range(lanes, chunk, lanes):
            out = op(out, part[:, at:at + lanes])
        return out

    def score(step, carry):
        base = pl.multiple_of(step * chunk, chunk)
        part = lax.dot_general(
            query[...], cache[which, :, pl.ds(base, chunk)], (((1,), (0,)), ((), ())),
            preferred_element_type=jnp.float32,
        )
        slot = base + lax.broadcasted_iota(jnp.int32, (1, chunk), 1)
        part = jnp.where(slot <= limit, part, -jnp.inf)
        scores[:, pl.ds(base, chunk)] = part
        peak_part[...] = jnp.maximum(peak_part[...], fold(part, jnp.maximum))
        return carry

    lax.fori_loop(0, ctx // chunk, score, 0)
    peak = jnp.max(peak_part[...], axis=1, keepdims=True) * coef

    def expo(step, carry):
        base = pl.multiple_of(step * chunk, chunk)
        part = jnp.exp2(scores[:, pl.ds(base, chunk)] * coef - peak)
        scores[:, pl.ds(base, chunk)] = part
        sum_part[...] += fold(part, jnp.add)
        return carry

    lax.fori_loop(0, ctx // chunk, expo, 0)
    inverse = 1.0 / jnp.sum(sum_part[...], axis=1, keepdims=True)

    def weigh(step, carry):
        base = pl.multiple_of(step * chunk, chunk)
        probs = (scores[:, pl.ds(base, chunk)] * inverse).astype(jnp.bfloat16)
        acc[...] += lax.dot_general(
            probs, cache[which, :kv, pl.ds(base, chunk)], (((1,), (1,)), ((), ())),
            preferred_element_type=jnp.float32,
        )
        return carry

    lax.fori_loop(0, ctx // chunk, weigh, 0)


def kernel(
    n, drafts, heads_here, nope, rope, kv, vd, coef, chunk,
    length_ref, start_ref, latent_ref, freq_ref, cache_hbm, wq_hbm, wk_hbm, wv_hbm,
    out_ref,
    cache, wq, wk, wv, gather, own_f32, q_full, wide_f32, rope_f32, send_q, send_r, recv_q, recv_r,
    query, scores, peak_part, sum_part, acc, send_o, recv_o,
    cache_sem, wq_sem, wk_sem, wv_sem, own_sem, ga_sem, gb_sem, gc_sem, ha_sem, hb_sem, hc_sem,
    sq_sem, sr_sem, so_sem, rq_sem, rr_sem, ro_sem,
):
    me = lax.axis_index("wide")
    owned = cache.shape[0]
    group = drafts * heads_here
    head_dim = nope + rope
    cores, lines, plane = gather.shape[:3]
    spots = lines * plane
    core, spot = lax.rem(me, cores), me // cores
    line, place = spot // plane, lax.rem(spot, plane)
    other = cores - 1 - core
    step, spot_step = spread_step(n), spread_step(spots)

    def partner(t):
        return lax.rem(me + lax.rem(t * step, n), n)

    load_q = pltpu.make_async_copy(wq_hbm, wq, wq_sem)
    load_k = pltpu.make_async_copy(wk_hbm, wk, wk_sem)
    load_v = pltpu.make_async_copy(wv_hbm, wv, wv_sem)
    loads = [
        pltpu.make_async_copy(cache_hbm.at[which], cache.at[which], cache_sem.at[which])
        for which in range(owned)
    ]
    barrier = pltpu.get_barrier_semaphore()

    def greet(t, carry):
        pl.semaphore_signal(barrier, inc=1, device_id={"wide": partner(t)}, device_id_type=MESH)
        return carry

    lax.fori_loop(1, n, greet, 0)
    load_q.start()
    load_k.start()
    for load in loads:
        load.start()
    load_v.start()

    for which in range(owned):
        own_f32[which * drafts:(which + 1) * drafts, :] = latent_ref[which].astype(jnp.float32)
    mine = own_f32[...]
    depth = mine.shape[1] // 2
    stacked = jnp.concatenate([mine[:, :depth], mine[:, depth:]], axis=0)
    gather[core, line, place] = stacked.astype(jnp.bfloat16)
    cosine, sine = rotary_tables(start_ref, freq_ref[...], drafts, group, rope, owned)
    pl.semaphore_wait(barrier, n - 1)

    def to_line(t, carry):
        there = lax.rem(line + t, lines)
        mine = gather.at[core, line, place]
        pltpu.make_async_remote_copy(
            src_ref=mine, dst_ref=mine, send_sem=ga_sem, recv_sem=ha_sem,
            device_id={"wide": (there * plane + place) * cores + core}, device_id_type=MESH,
        ).start()
        return carry

    def to_plane(t, carry):
        there = lax.rem(place + t, plane)
        mine = gather.at[core, :, place]
        pltpu.make_async_remote_copy(
            src_ref=mine, dst_ref=mine, send_sem=gb_sem, recv_sem=hb_sem,
            device_id={"wide": (line * plane + there) * cores + core}, device_id_type=MESH,
        ).start()
        return carry

    def landed(ref, sem):
        pltpu.make_async_copy(ref, ref, sem).wait()

    lax.fori_loop(1, lines, to_line, 0)
    landed(gather.at[core, pl.ds(0, lines - 1), place], ha_sem)
    lax.fori_loop(1, plane, to_plane, 0)
    landed(gather.at[core, :, pl.ds(0, plane - 1)], hb_sem)
    across = pltpu.make_async_remote_copy(
        src_ref=gather.at[core], dst_ref=gather.at[core], send_sem=gc_sem, recv_sem=hc_sem,
        device_id={"wide": spot * cores + other}, device_id_type=MESH,
    )
    across.start()

    def queries(side):
        rows = q_full.shape[0]
        latents = gather[side].reshape(spots, 2 * owned * drafts, depth).astype(jnp.float32)
        low = latents[:, :owned * drafts].reshape(rows, depth).astype(jnp.bfloat16)
        high = latents[:, owned * drafts:].reshape(rows, depth).astype(jnp.bfloat16)
        columns = heads_here * head_dim
        block = 256 if columns % 256 == 0 else columns
        for at in range(0, columns, block):
            part = jnp.dot(low, wq[:depth, at:at + block], preferred_element_type=jnp.float32)
            part += jnp.dot(high, wq[depth:, at:at + block], preferred_element_type=jnp.float32)
            q_full[:, at:at + block] = part.astype(jnp.bfloat16).astype(jnp.float32)
        for head in range(heads_here):
            at = head * head_dim
            absorbed = jnp.dot(
                q_full[:, at:at + nope].astype(jnp.bfloat16), wk[head],
                preferred_element_type=jnp.float32,
            )
            for part in range(kv // 128):
                wide_f32[part, pl.ds(head, rows, stride=heads_here), :] = absorbed[:, part * 128:part * 128 + 128]
            tail = q_full[:, at + nope:at + head_dim]
            rope_f32[pl.ds(head, rows, stride=heads_here), :] = jnp.concatenate([tail] * owned, axis=-1)
        for part in range(kv // 128):
            packed = wide_f32[part, :rows * heads_here].astype(jnp.bfloat16).reshape(spots, owned, group, 128)
            for which in range(owned):
                send_q[side, which, :, :, part * 128:part * 128 + 128] = packed[:, which]
        turned = rope_f32[:, :rope].reshape(spots, owned, group, rope)
        send_r[side] = jnp.concatenate(
            [turned[:, which] for which in range(owned)], axis=-1
        ).astype(jnp.bfloat16)

    def post(t, carry, which, side):
        there = lax.rem(spot + lax.rem(t * spot_step, spots), spots)
        target = {"wide": there * cores + side}
        if which == 0:
            pltpu.make_async_remote_copy(
                src_ref=send_r.at[side, there], dst_ref=recv_r.at[me], send_sem=sr_sem, recv_sem=rr_sem,
                device_id=target, device_id_type=MESH,
            ).start()
        pltpu.make_async_remote_copy(
            src_ref=send_q.at[side, which, there], dst_ref=recv_q.at[which, me],
            send_sem=sq_sem.at[which], recv_sem=rq_sem.at[which],
            device_id=target, device_id_type=MESH,
        ).start()
        return carry

    load_q.wait()
    load_k.wait()
    queries(core)
    lax.fori_loop(1, spots, functools.partial(post, which=0, side=core), 0)
    across.wait_recv()
    queries(other)
    lax.fori_loop(0, spots, functools.partial(post, which=0, side=other), 0)
    for which in range(1, owned):
        lax.fori_loop(1, spots, functools.partial(post, which=which, side=core), 0)
        lax.fori_loop(0, spots, functools.partial(post, which=which, side=other), 0)
    keep = [
        pltpu.make_async_copy(send_q.at[core, which, spot], recv_q.at[which, me], own_sem.at[which])
        for which in range(owned)
    ] + [pltpu.make_async_copy(send_r.at[core, spot], recv_r.at[me], own_sem.at[owned])]
    for copy in keep:
        copy.start()
    for copy in keep:
        copy.wait()

    def all_but_one(ref, sem):
        pltpu.make_async_copy(ref.at[pl.ds(0, n - 1)], ref.at[pl.ds(0, n - 1)], sem).wait()

    def post_out(t, carry, which):
        d = partner(t)
        pltpu.make_async_remote_copy(
            src_ref=send_o.at[which, d], dst_ref=recv_o.at[which, me],
            send_sem=so_sem.at[which], recv_sem=ro_sem.at[which],
            device_id={"wide": d}, device_id_type=MESH,
        ).start()
        return carry

    all_but_one(recv_r, rr_sem)
    turn = recv_r[...].astype(jnp.float32)
    width = turn.shape[2]
    flat = turn.reshape(n * group, width)
    lane = lax.broadcasted_iota(jnp.int32, (1, width), 1)
    half = rope // 2
    swapped = jnp.where(
        lax.rem(lane, rope) < half,
        pltpu.roll(flat, width - half, 1),
        pltpu.roll(flat, half, 1),
    ).reshape(n, group, width)
    rotated = (turn * cosine[None] + swapped * sine[None]).reshape(n * group, width)
    rope_f32[:n * group, :] = rotated

    for which in range(owned):
        all_but_one(recv_q.at[which], rq_sem.at[which])
        query[:, :kv] = recv_q[which].reshape(n * group, kv)
        query[:, kv:] = rope_f32[:n * group, which * rope:(which + 1) * rope].astype(jnp.bfloat16)
        loads[which].wait()
        attend(
            which, length_ref[which], query, cache, scores, peak_part, sum_part, acc,
            drafts, group, kv, coef, chunk,
        )
        send_o[which] = acc[...].astype(jnp.bfloat16).reshape(n, group, kv)
        lax.fori_loop(1, n, functools.partial(post_out, which=which), 0)
        own = pltpu.make_async_copy(send_o.at[which, me], recv_o.at[which, me], own_sem.at[0])
        own.start()
        own.wait()

    load_v.wait()
    rows = out_ref.shape[0]
    for which in range(owned):
        all_but_one(recv_o.at[which], ro_sem.at[which])
    for part in range(kv // 128):
        lanes = slice(part * 128, part * 128 + 128)
        arrived = jnp.stack([recv_o[which, :, :, lanes] for which in range(owned)], axis=1)
        wide_f32[part] = arrived.astype(jnp.float32).reshape(n * owned * group, 128)
    for head in range(heads_here):
        mine = jnp.concatenate(
            [wide_f32[part, pl.ds(head, rows, stride=heads_here), :] for part in range(kv // 128)], axis=-1
        ).astype(jnp.bfloat16)
        out_ref[:, head * vd:(head + 1) * vd] = jnp.dot(
            mine, wv[head], preferred_element_type=jnp.float32
        ).astype(jnp.bfloat16)

    landed(gather.at[core, pl.ds(0, lines - 1), place], ga_sem)
    landed(gather.at[core, :, pl.ds(0, plane - 1)], gb_sem)
    across.wait_send()
    all_but_one(recv_r, sr_sem)
    for which in range(owned):
        all_but_one(recv_q.at[which], sq_sem.at[which])
        all_but_one(send_o.at[which], so_sem.at[which])


def per_device(q_latent, draft_start, cache_len, latent_cache, w_q_up, w_k_absorb, value_up_weight):
    n = lax.axis_size("wide")
    heads_here, nope, kv = w_k_absorb.shape
    vd = value_up_weight.shape[2]
    head_dim = w_q_up.shape[1] // heads_here
    rope = head_dim - nope
    owned, ctx, width = latent_cache.shape[1:]
    drafts, ql = q_latent.shape[2:]
    group = drafts * heads_here
    rows = n * owned * drafts
    chunk = min(512, ctx)
    coef = float(head_dim) ** -0.5 * math.log2(math.e)
    bf16, f32 = jnp.bfloat16, jnp.float32

    wq = lax.all_gather(w_q_up, "batch", axis=0, tiled=True)
    freqs = 10000.0 ** (-jnp.arange(rope // 2).astype(f32) * 2.0 / rope)
    freqs = jnp.tile(freqs, 2 * owned)[None]
    cores, plane = 2, 4
    spots, lines = n // cores, n // (cores * plane)

    vmem = pl.BlockSpec(memory_space=pltpu.VMEM)
    smem = pl.BlockSpec(memory_space=pltpu.SMEM)
    hbm = pl.BlockSpec(memory_space=pl.ANY)
    dma = pltpu.SemaphoreType.DMA
    out = pl.pallas_call(
        functools.partial(kernel, n, drafts, heads_here, nope, rope, kv, vd, coef, chunk),
        out_shape=jax.ShapeDtypeStruct((rows, heads_here * vd), bf16),
        in_specs=[smem, smem, vmem, vmem, hbm, hbm, hbm, hbm],
        out_specs=vmem,
        scratch_shapes=[
            pltpu.VMEM((owned, width, ctx), bf16),
            pltpu.VMEM(wq.shape, bf16),
            pltpu.VMEM(w_k_absorb.shape, bf16),
            pltpu.VMEM(value_up_weight.shape, bf16),
            pltpu.VMEM((cores, lines, plane, 2 * owned * drafts, ql // 2), bf16),
            pltpu.VMEM((owned * drafts, ql), f32),
            pltpu.VMEM((rows // cores, heads_here * head_dim), f32),
            pltpu.VMEM((kv // 128, rows * heads_here, 128), f32),
            pltpu.VMEM((rows * heads_here // cores, owned * rope), f32),
            pltpu.VMEM((cores, owned, spots, group, kv), bf16),
            pltpu.VMEM((cores, spots, group, owned * rope), bf16),
            pltpu.VMEM((owned, n, group, kv), bf16),
            pltpu.VMEM((n, group, owned * rope), bf16),
            pltpu.VMEM((n * group, width), bf16),
            pltpu.VMEM((n * group, ctx), f32),
            pltpu.VMEM((n * group, min(128, chunk)), f32),
            pltpu.VMEM((n * group, min(128, chunk)), f32),
            pltpu.VMEM((n * group, kv), f32),
            pltpu.VMEM((owned, n, group, kv), bf16),
            pltpu.VMEM((owned, n, group, kv), bf16),
            dma((owned,)), dma, dma, dma, dma((owned + 1,)), dma, dma, dma, dma, dma, dma,
            dma((owned,)), dma, dma((owned,)), dma((owned,)), dma, dma((owned,)),
        ],
        compiler_params=pltpu.CompilerParams(
            collective_id=0, has_side_effects=True, vmem_limit_bytes=56 << 20
        ),
    )(cache_len[0], draft_start[0], q_latent[0], freqs, jnp.swapaxes(latent_cache[0], 1, 2), wq, w_k_absorb, value_up_weight)
    return out.reshape(1, n * owned, drafts, heads_here * vd)


def solution(mesh):
    in_specs = (
        P("batch", "wide", None, None),
        P("batch", "wide"),
        P("batch", "wide"),
        P("batch", "wide", None, None),
        P("batch", "wide"),
        P("wide", None, None),
        P("wide", None, None),
    )
    out_specs = P("batch", None, None, "wide")
    return jax.shard_map(
        per_device, mesh=mesh, in_specs=in_specs, out_specs=out_specs, check_vma=False
    )
```

time: 127 us -> 78.2 us (0.62)
  the two profiles are of different devices: /device:TPU:0 before, /device:TPU:1 now
where the time goes in v2:
time: 78.2 us; the launch traced here: 76.7 us
  Pallas kernels  74.4 us (95%)
  local copies, waits for them, and re-layouts  2.32 us (3%)
    pallas_call x1, Pallas kernels, per_device(): pl.pallas_call(functools.partial(kernel, n, drafts, heads_here, nope, rop...  74.4 us
    reshape x1, local copies, waits for them, and re-layouts, per_device(): return out.reshape(1, n * owned, drafts, heads_here * vd)  1.72 us

profile of v2, /device:TPU:1, one launch (start us, length us, event | category | flops | bytes accessed | tf_op | source)
XLA Modules:
  0.0 76.7 jit_solution(8620634159858143036)
XLA Ops:
  0.0 0.6 broadcast_in_dim_tile.3.freq_ref
  0.6 74.4 %shard_map.73 = bf16[256,512]{1,0:T(8,128)(2,1)} custom-call(s32[2]{0:T(128)} %bitcast.8, s32[2]{0:T(128)} %bitcast.9, bf16[2,4,1536]{2,1,0:T(4,128)(2,1)} %bitcast.7, f32[1,128]{1,0:T(1,128)} %broadcast_in_dim_tile.3.freq_ref, bf16[2,576,4096]{2,1,0:T(8,128)(2,1)} %bitcast.6, bf16[1536,768]{1,0:T(8,128)(2,1)} %wq_hbm, bf16[4,128,512]{2,1,0:T(8,128)(2,1)} %wk_hbm.1, ...), custom_call_target="tpu_custom_call" | custom-call | tf_op jit(solution)/shard_map/pallas_call | solution.py:327
  75.0 1.7 %reshape.10 = bf16[1,64,4,512]{3,2,1,0:T(4,128)(2,1)} reshape(bf16[256,512]{1,0:T(8,128)(2,1)} %shard_map.73) | data formatting | bytes 524288 | tf_op jit(solution)/shard_map/reshape | solution.py:360
  (2 shorter events, 0.0 us)

commit v3 on v2

--- a/solution.py
+++ b/solution.py
@@ -2,6 +2,7 @@
 import math
 import jax
 import jax.numpy as jnp
+import numpy as np
 from jax import lax
 from jax.experimental import pallas as pl
 from jax.experimental.pallas import tpu as pltpu
@@ -17,10 +18,15 @@
     return step
 
 
-def rotary_tables(start_ref, freq, drafts, group, rope_width, owned):
+def rotary_tables(start_ref, drafts, group, rope_width, owned):
     shape = (group, owned * rope_width)
     row = lax.broadcasted_iota(jnp.int32, shape, 0) // (group // drafts)
     lane = lax.broadcasted_iota(jnp.int32, shape, 1)
+    half = rope_width // 2
+    freqs = 10000.0 ** (-np.arange(half) * 2.0 / rope_width)
+    freq = jnp.zeros(shape, jnp.float32)
+    for at in range(half):
+        freq = jnp.where(lax.rem(lane, half) == at, np.float32(freqs[at]), freq)
     start = jnp.full(shape, start_ref[0], jnp.int32)
     for which in range(1, owned):
         start = jnp.where(lane // rope_width == which, start_ref[which], start)
@@ -52,9 +58,8 @@
 
     def score(step, carry):
         base = pl.multiple_of(step * chunk, chunk)
-        part = lax.dot_general(
-            query[...], cache[which, :, pl.ds(base, chunk)], (((1,), (0,)), ((), ())),
-            preferred_element_type=jnp.float32,
+        part = jnp.dot(
+            query[...], cache[which, :, pl.ds(base, chunk)], preferred_element_type=jnp.float32
         )
         slot = base + lax.broadcasted_iota(jnp.int32, (1, chunk), 1)
         part = jnp.where(slot <= limit, part, -jnp.inf)
@@ -65,33 +70,25 @@
     lax.fori_loop(0, ctx // chunk, score, 0)
     peak = jnp.max(peak_part[...], axis=1, keepdims=True) * coef
 
-    def expo(step, carry):
+    def weigh(step, carry):
         base = pl.multiple_of(step * chunk, chunk)
         part = jnp.exp2(scores[:, pl.ds(base, chunk)] * coef - peak)
-        scores[:, pl.ds(base, chunk)] = part
         sum_part[...] += fold(part, jnp.add)
-        return carry
-
-    lax.fori_loop(0, ctx // chunk, expo, 0)
-    inverse = 1.0 / jnp.sum(sum_part[...], axis=1, keepdims=True)
-
-    def weigh(step, carry):
-        base = pl.multiple_of(step * chunk, chunk)
-        probs = (scores[:, pl.ds(base, chunk)] * inverse).astype(jnp.bfloat16)
         acc[...] += lax.dot_general(
-            probs, cache[which, :kv, pl.ds(base, chunk)], (((1,), (1,)), ((), ())),
-            preferred_element_type=jnp.float32,
+            part.astype(jnp.bfloat16), cache[which, :kv, pl.ds(base, chunk)],
+            (((1,), (1,)), ((), ())), preferred_element_type=jnp.float32,
         )
         return carry
 
     lax.fori_loop(0, ctx // chunk, weigh, 0)
+    return acc[...] * (1.0 / jnp.sum(sum_part[...], axis=1, keepdims=True))
 
 
 def kernel(
     n, drafts, heads_here, nope, rope, kv, vd, coef, chunk,
-    length_ref, start_ref, latent_ref, freq_ref, cache_hbm, wq_hbm, wk_hbm, wv_hbm,
+    length_ref, start_ref, latent_ref, cache_hbm, wq_hbm, wk_hbm, wv_hbm,
     out_ref,
-    cache, wq, wk, wv, gather, own_f32, q_full, wide_f32, rope_f32, send_q, send_r, recv_q, recv_r,
+    cache, wq, wk, wv, gather, own_f32, q_full, wide_f32, rope_f32, turned_f32, send_q, send_r, recv_q, recv_r,
     query, scores, peak_part, sum_part, acc, send_o, recv_o,
     cache_sem, wq_sem, wk_sem, wv_sem, own_sem, ga_sem, gb_sem, gc_sem, ha_sem, hb_sem, hc_sem,
     sq_sem, sr_sem, so_sem, rq_sem, rr_sem, ro_sem,
@@ -136,7 +133,7 @@
     depth = mine.shape[1] // 2
     stacked = jnp.concatenate([mine[:, :depth], mine[:, depth:]], axis=0)
     gather[core, line, place] = stacked.astype(jnp.bfloat16)
-    cosine, sine = rotary_tables(start_ref, freq_ref[...], drafts, group, rope, owned)
+    cosine, sine = rotary_tables(start_ref, drafts, group, rope, owned)
     pl.semaphore_wait(barrier, n - 1)
 
     def to_line(t, carry):
@@ -200,104 +197,123 @@
             [turned[:, which] for which in range(owned)], axis=-1
         ).astype(jnp.bfloat16)
 
-    def post(t, carry, which, side):
-        there = lax.rem(spot + lax.rem(t * spot_step, spots), spots)
-        target = {"wide": there * cores + side}
+    sides = (core, other)
+
+    def blocks(ref, kind):
+        return ref.at[pl.ds(0, spots - 1)] if kind == 0 else ref
+
+    def ship(source, sink, send_sem, recv_sem, kind):
+        side = sides[kind]
+
+        def post(t, carry):
+            there = lax.rem(spot + lax.rem(t * spot_step, spots), spots)
+            pltpu.make_async_remote_copy(
+                src_ref=source.at[there], dst_ref=sink.at[core, spot],
+                send_sem=send_sem, recv_sem=recv_sem,
+                device_id={"wide": there * cores + side}, device_id_type=MESH,
+            ).start()
+            return carry
+
+        lax.fori_loop(1 - kind, spots, post, 0)
+
+    def ship_queries(which, kind):
+        side = sides[kind]
         if which == 0:
-            pltpu.make_async_remote_copy(
-                src_ref=send_r.at[side, there], dst_ref=recv_r.at[me], send_sem=sr_sem, recv_sem=rr_sem,
-                device_id=target, device_id_type=MESH,
-            ).start()
-        pltpu.make_async_remote_copy(
-            src_ref=send_q.at[side, which, there], dst_ref=recv_q.at[which, me],
-            send_sem=sq_sem.at[which], recv_sem=rq_sem.at[which],
-            device_id=target, device_id_type=MESH,
-        ).start()
-        return carry
-
+            ship(send_r.at[side], recv_r, sr_sem.at[kind], rr_sem.at[kind], kind)
+        ship(
+            send_q.at[side, which], recv_q.at[which],
+            sq_sem.at[which, kind], rq_sem.at[which, kind], kind,
+        )
+
+    def settle(ref, sem, kind):
+        landed(blocks(ref, kind), sem)
+
+    pieces = [(which, kind) for which in range(owned) for kind in range(2)]
     load_q.wait()
     load_k.wait()
     queries(core)
-    lax.fori_loop(1, spots, functools.partial(post, which=0, side=core), 0)
+    ship_queries(0, 0)
     across.wait_recv()
     queries(other)
-    lax.fori_loop(0, spots, functools.partial(post, which=0, side=other), 0)
-    for which in range(1, owned):
-        lax.fori_loop(1, spots, functools.partial(post, which=which, side=core), 0)
-        lax.fori_loop(0, spots, functools.partial(post, which=which, side=other), 0)
+    ship_queries(0, 1)
     keep = [
-        pltpu.make_async_copy(send_q.at[core, which, spot], recv_q.at[which, me], own_sem.at[which])
+        pltpu.make_async_copy(send_q.at[core, which, spot], recv_q.at[which, core, spot], own_sem.at[which])
         for which in range(owned)
-    ] + [pltpu.make_async_copy(send_r.at[core, spot], recv_r.at[me], own_sem.at[owned])]
+    ] + [pltpu.make_async_copy(send_r.at[core, spot], recv_r.at[core, spot], own_sem.at[owned])]
     for copy in keep:
         copy.start()
     for copy in keep:
         copy.wait()
 
-    def all_but_one(ref, sem):
-        pltpu.make_async_copy(ref.at[pl.ds(0, n - 1)], ref.at[pl.ds(0, n - 1)], sem).wait()
-
-    def post_out(t, carry, which):
-        d = partner(t)
-        pltpu.make_async_remote_copy(
-            src_ref=send_o.at[which, d], dst_ref=recv_o.at[which, me],
-            send_sem=so_sem.at[which], recv_sem=ro_sem.at[which],
-            device_id={"wide": d}, device_id_type=MESH,
-        ).start()
-        return carry
-
-    all_but_one(recv_r, rr_sem)
-    turn = recv_r[...].astype(jnp.float32)
-    width = turn.shape[2]
-    flat = turn.reshape(n * group, width)
-    lane = lax.broadcasted_iota(jnp.int32, (1, width), 1)
-    half = rope // 2
-    swapped = jnp.where(
-        lax.rem(lane, rope) < half,
-        pltpu.roll(flat, width - half, 1),
-        pltpu.roll(flat, half, 1),
-    ).reshape(n, group, width)
-    rotated = (turn * cosine[None] + swapped * sine[None]).reshape(n * group, width)
-    rope_f32[:n * group, :] = rotated
-
-    for which in range(owned):
-        all_but_one(recv_q.at[which], rq_sem.at[which])
-        query[:, :kv] = recv_q[which].reshape(n * group, kv)
-        query[:, kv:] = rope_f32[:n * group, which * rope:(which + 1) * rope].astype(jnp.bfloat16)
-        loads[which].wait()
-        attend(
+    def turn_queries(kind):
+        settle(recv_r.at[sides[kind]], rr_sem.at[kind], kind)
+        turn = recv_r[sides[kind]].astype(jnp.float32)
+        width = turn.shape[2]
+        flat = turn.reshape(spots * group, width)
+        lane = lax.broadcasted_iota(jnp.int32, (1, width), 1)
+        half = rope // 2
+        swapped = jnp.where(
+            lax.rem(lane, rope) < half,
+            pltpu.roll(flat, width - half, 1),
+            pltpu.roll(flat, half, 1),
+        ).reshape(spots, group, width)
+        rotated = turn * cosine[None] + swapped * sine[None]
+        turned_f32[kind] = rotated.reshape(spots * group, width)
+
+    for number, (which, kind) in enumerate(pieces):
+        side = sides[kind]
+        if number + 2 < len(pieces):
+            settle(send_q.at[side, which], sq_sem.at[which, kind], kind)
+            ship_queries(*pieces[number + 2])
+        if which == 0:
+            turn_queries(kind)
+        settle(recv_q.at[which, side], rq_sem.at[which, kind], kind)
+        query[:, :kv] = recv_q[which, side].reshape(spots * group, kv)
+        query[:, kv:] = turned_f32[kind, :, which * rope:(which + 1) * rope].astype(jnp.bfloat16)
+        if kind == 0:
+            loads[which].wait()
+        latents = attend(
             which, length_ref[which], query, cache, scores, peak_part, sum_part, acc,
             drafts, group, kv, coef, chunk,
         )
-        send_o[which] = acc[...].astype(jnp.bfloat16).reshape(n, group, kv)
-        lax.fori_loop(1, n, functools.partial(post_out, which=which), 0)
-        own = pltpu.make_async_copy(send_o.at[which, me], recv_o.at[which, me], own_sem.at[0])
-        own.start()
-        own.wait()
+        send_o[which, side] = latents.astype(jnp.bfloat16).reshape(spots, group, kv)
+        ship(
+            send_o.at[which, side], recv_o.at[which],
+            so_sem.at[which, kind], ro_sem.at[which, kind], kind,
+        )
+        if kind == 0:
+            own = pltpu.make_async_copy(
+                send_o.at[which, core, spot], recv_o.at[which, core, spot], own_sem.at[0]
+            )
+            own.start()
+            own.wait()
 
     load_v.wait()
-    rows = out_ref.shape[0]
-    for which in range(owned):
-        all_but_one(recv_o.at[which], ro_sem.at[which])
-    for part in range(kv // 128):
-        lanes = slice(part * 128, part * 128 + 128)
-        arrived = jnp.stack([recv_o[which, :, :, lanes] for which in range(owned)], axis=1)
-        wide_f32[part] = arrived.astype(jnp.float32).reshape(n * owned * group, 128)
-    for head in range(heads_here):
-        mine = jnp.concatenate(
-            [wide_f32[part, pl.ds(head, rows, stride=heads_here), :] for part in range(kv // 128)], axis=-1
-        ).astype(jnp.bfloat16)
-        out_ref[:, head * vd:(head + 1) * vd] = jnp.dot(
-            mine, wv[head], preferred_element_type=jnp.float32
-        ).astype(jnp.bfloat16)
+    rows = spots * drafts
+    for which, kind in pieces:
+        side = sides[kind]
+        settle(recv_o.at[which, side], ro_sem.at[which, kind], kind)
+        for part in range(kv // 128):
+            arrived = recv_o[which, side, :, :, part * 128:part * 128 + 128]
+            wide_f32[part, :spots * group] = arrived.astype(jnp.float32).reshape(spots * group, 128)
+        for head in range(heads_here):
+            mine = jnp.concatenate(
+                [wide_f32[part, pl.ds(head, rows, stride=heads_here), :] for part in range(kv // 128)], axis=-1
+            ).astype(jnp.bfloat16)
+            value = jnp.dot(mine, wv[head], preferred_element_type=jnp.float32)
+            out_ref[:, side, which, :, head * vd:(head + 1) * vd] = value.reshape(
+                spots, drafts, vd
+            ).astype(jnp.bfloat16)
 
     landed(gather.at[core, pl.ds(0, lines - 1), place], ga_sem)
     landed(gather.at[core, :, pl.ds(0, plane - 1)], gb_sem)
     across.wait_send()
-    all_but_one(recv_r, sr_sem)
-    for which in range(owned):
-        all_but_one(recv_q.at[which], sq_sem.at[which])
-        all_but_one(send_o.at[which], so_sem.at[which])
+    for kind in range(2):
+        settle(send_r.at[sides[kind]], sr_sem.at[kind], kind)
+    for number, (which, kind) in enumerate(pieces):
+        if number + 2 >= len(pieces):
+            settle(send_q.at[sides[kind], which], sq_sem.at[which, kind], kind)
+        settle(send_o.at[which, sides[kind]], so_sem.at[which, kind], kind)
 
 
 def per_device(q_latent, draft_start, cache_len, latent_cache, w_q_up, w_k_absorb, value_up_weight):
@@ -310,13 +326,11 @@
     drafts, ql = q_latent.shape[2:]
     group = drafts * heads_here
     rows = n * owned * drafts
-    chunk = min(512, ctx)
+    chunk = min(1024, ctx)
     coef = float(head_dim) ** -0.5 * math.log2(math.e)
     bf16, f32 = jnp.bfloat16, jnp.float32
 
     wq = lax.all_gather(w_q_up, "batch", axis=0, tiled=True)
-    freqs = 10000.0 ** (-jnp.arange(rope // 2).astype(f32) * 2.0 / rope)
-    freqs = jnp.tile(freqs, 2 * owned)[None]
     cores, plane = 2, 4
     spots, lines = n // cores, n // (cores * plane)
 
@@ -326,8 +340,8 @@
     dma = pltpu.SemaphoreType.DMA
     out = pl.pallas_call(
         functools.partial(kernel, n, drafts, heads_here, nope, rope, kv, vd, coef, chunk),
-        out_shape=jax.ShapeDtypeStruct((rows, heads_here * vd), bf16),
-        in_specs=[smem, smem, vmem, vmem, hbm, hbm, hbm, hbm],
+        out_shape=jax.ShapeDtypeStruct((spots, cores, owned, drafts, heads_here * vd), bf16),
+        in_specs=[smem, smem, vmem, hbm, hbm, hbm, hbm],
         out_specs=vmem,
         scratch_shapes=[
             pltpu.VMEM((owned, width, ctx), bf16),
@@ -337,26 +351,28 @@
             pltpu.VMEM((cores, lines, plane, 2 * owned * drafts, ql // 2), bf16),
             pltpu.VMEM((owned * drafts, ql), f32),
             pltpu.VMEM((rows // cores, heads_here * head_dim), f32),
-            pltpu.VMEM((kv // 128, rows * heads_here, 128), f32),
+            pltpu.VMEM((kv // 128, rows * heads_here // cores, 128), f32),
             pltpu.VMEM((rows * heads_here // cores, owned * rope), f32),
+            pltpu.VMEM((cores, spots * group, owned * rope), f32),
             pltpu.VMEM((cores, owned, spots, group, kv), bf16),
             pltpu.VMEM((cores, spots, group, owned * rope), bf16),
-            pltpu.VMEM((owned, n, group, kv), bf16),
-            pltpu.VMEM((n, group, owned * rope), bf16),
-            pltpu.VMEM((n * group, width), bf16),
-            pltpu.VMEM((n * group, ctx), f32),
-            pltpu.VMEM((n * group, min(128, chunk)), f32),
-            pltpu.VMEM((n * group, min(128, chunk)), f32),
-            pltpu.VMEM((n * group, kv), f32),
-            pltpu.VMEM((owned, n, group, kv), bf16),
-            pltpu.VMEM((owned, n, group, kv), bf16),
+            pltpu.VMEM((owned, cores, spots, group, kv), bf16),
+            pltpu.VMEM((cores, spots, group, owned * rope), bf16),
+            pltpu.VMEM((spots * group, width), bf16),
+            pltpu.VMEM((spots * group, ctx), f32),
+            pltpu.VMEM((spots * group, min(128, chunk)), f32),
+            pltpu.VMEM((spots * group, min(128, chunk)), f32),
+            pltpu.VMEM((spots * group, kv), f32),
+            pltpu.VMEM((owned, cores, spots, group, kv), bf16),
+            pltpu.VMEM((owned, cores, spots, group, kv), bf16),
             dma((owned,)), dma, dma, dma, dma((owned + 1,)), dma, dma, dma, dma, dma, dma,
-            dma((owned,)), dma, dma((owned,)), dma((owned,)), dma, dma((owned,)),
+            dma((owned, cores)), dma((cores,)), dma((owned, cores)),
+            dma((owned, cores)), dma((cores,)), dma((owned, cores)),
         ],
         compiler_params=pltpu.CompilerParams(
             collective_id=0, has_side_effects=True, vmem_limit_bytes=56 << 20
         ),
-    )(cache_len[0], draft_start[0], q_latent[0], freqs, jnp.swapaxes(latent_cache[0], 1, 2), wq, w_k_absorb, value_up_weight)
+    )(cache_len[0], draft_start[0], q_latent[0], jnp.swapaxes(latent_cache[0], 1, 2), wq, w_k_absorb, value_up_weight)
     return out.reshape(1, n * owned, drafts, heads_here * vd)
 
 

time: 78.2 us -> 70.9 us (0.907); the launches traced: 76.7 us -> 70.5 us
  Pallas kernels: 74.4 us -> 68.8 us
    pallas_call x1, Pallas kernels: 74.4 us -> 68.8 us  [per_device(): pl.pallas_call(functools.partial(kernel, n, drafts, heads_here, nope, rop...]
    unnamed x0 -> x1, local copies, waits for them, and re-layouts: none -> 1.74 us
    reshape x1 -> x0, local copies, waits for them, and re-layouts: 1.72 us -> none  [per_device(): return out.reshape(1, n * owned, drafts, heads_here * vd)]
where the time goes in v3:
time: 70.9 us; the launch traced here: 70.5 us
  Pallas kernels  68.8 us (97%)
  local copies, waits for them, and re-layouts  1.74 us (2%)
    pallas_call x1, Pallas kernels, per_device(): pl.pallas_call(functools.partial(kernel, n, drafts, heads_here, nope, rop...  68.8 us
    unnamed x1, local copies, waits for them, and re-layouts  1.74 us

profile of v3, /device:TPU:1, one launch (start us, length us, event | category | flops | bytes accessed | tf_op | source)
XLA Modules:
  0.0 70.5 jit_solution(9041037374476714074)
XLA Ops:
  0.0 68.8 %shard_map.73 = bf16[16,2,2,4,512]{4,3,2,1,0:T(4,128)(2,1)} custom-call(s32[2]{0:T(128)} %bitcast.10, s32[2]{0:T(128)} %bitcast.11, bf16[2,4,1536]{2,1,0:T(4,128)(2,1)} %bitcast.9, bf16[2,576,4096]{2,1,0:T(8,128)(2,1)} %bitcast.7, bf16[1536,768]{1,0:T(8,128)(2,1)} %wq_hbm, bf16[4,128,512]{2,1,0:T(8,128)(2,1)} %wk_hbm.1, bf16[4,512,128]{2,1,0:T(8,128)(2,1)} %wv_hbm.1), custom_call_target="tpu_custom_call" | custom-call | tf_op jit(solution)/shard_map/pallas_call | solution.py:341
  68.8 1.7 %copy.9 = bf16[1,64,4,512]{3,2,1,0:T(4,128)(2,1)} copy(bf16[1,64,4,512]{3,2,1,0:T(4,128)(2,1)} %bitcast.8) | data formatting | bytes 524288

commit v4 on v3

--- a/solution.py
+++ b/solution.py
@@ -88,10 +88,10 @@
     n, drafts, heads_here, nope, rope, kv, vd, coef, chunk,
     length_ref, start_ref, latent_ref, cache_hbm, wq_hbm, wk_hbm, wv_hbm,
     out_ref,
-    cache, wq, wk, wv, gather, own_f32, q_full, wide_f32, rope_f32, turned_f32, send_q, send_r, recv_q, recv_r,
+    cache, wq, wk, wv, gather, own_f32, q_full, wide_f32, rope_f32, turned_f32, send_first, send_q, recv_first, recv_q,
     query, scores, peak_part, sum_part, acc, send_o, recv_o,
     cache_sem, wq_sem, wk_sem, wv_sem, own_sem, ga_sem, gb_sem, gc_sem, ha_sem, hb_sem, hc_sem,
-    sq_sem, sr_sem, so_sem, rq_sem, rr_sem, ro_sem,
+    sq_sem, so_sem, rq_sem, ro_sem,
 ):
     me = lax.axis_index("wide")
     owned = cache.shape[0]
@@ -136,36 +136,43 @@
     cosine, sine = rotary_tables(start_ref, drafts, group, rope, owned)
     pl.semaphore_wait(barrier, n - 1)
 
-    def to_line(t, carry):
+    def to_line(t):
         there = lax.rem(line + t, lines)
         mine = gather.at[core, line, place]
         pltpu.make_async_remote_copy(
-            src_ref=mine, dst_ref=mine, send_sem=ga_sem, recv_sem=ha_sem,
+            src_ref=mine, dst_ref=mine, send_sem=ga_sem, recv_sem=ha_sem.at[t],
             device_id={"wide": (there * plane + place) * cores + core}, device_id_type=MESH,
         ).start()
-        return carry
-
-    def to_plane(t, carry):
-        there = lax.rem(place + t, plane)
-        mine = gather.at[core, :, place]
-        pltpu.make_async_remote_copy(
-            src_ref=mine, dst_ref=mine, send_sem=gb_sem, recv_sem=hb_sem,
-            device_id={"wide": (line * plane + there) * cores + core}, device_id_type=MESH,
-        ).start()
-        return carry
+
+    def to_plane(source):
+        block = gather.at[core, source, place]
+        for t in range(1, plane):
+            there = lax.rem(place + t, plane)
+            pltpu.make_async_remote_copy(
+                src_ref=block, dst_ref=block, send_sem=gb_sem, recv_sem=hb_sem,
+                device_id={"wide": (line * plane + there) * cores + core}, device_id_type=MESH,
+            ).start()
 
     def landed(ref, sem):
         pltpu.make_async_copy(ref, ref, sem).wait()
 
-    lax.fori_loop(1, lines, to_line, 0)
-    landed(gather.at[core, pl.ds(0, lines - 1), place], ha_sem)
-    lax.fori_loop(1, plane, to_plane, 0)
+    nearest = sorted(range(1, lines), key=lambda t: min(t, lines - t))
+    for t in nearest[::-1]:
+        to_line(t)
+    to_plane(line)
+    for t in nearest:
+        source = lax.rem(line + lines - t, lines)
+        landed(gather.at[core, source, place], ha_sem.at[t])
+        to_plane(source)
     landed(gather.at[core, :, pl.ds(0, plane - 1)], hb_sem)
     across = pltpu.make_async_remote_copy(
         src_ref=gather.at[core], dst_ref=gather.at[core], send_sem=gc_sem, recv_sem=hc_sem,
         device_id={"wide": spot * cores + other}, device_id_type=MESH,
     )
     across.start()
+
+    sends = [send_first] + [send_q.at[which] for which in range(owned - 1)]
+    recvs = [recv_first] + [recv_q.at[which] for which in range(owned - 1)]
 
     def queries(side):
         rows = q_full.shape[0]
@@ -191,9 +198,9 @@
         for part in range(kv // 128):
             packed = wide_f32[part, :rows * heads_here].astype(jnp.bfloat16).reshape(spots, owned, group, 128)
             for which in range(owned):
-                send_q[side, which, :, :, part * 128:part * 128 + 128] = packed[:, which]
+                sends[which][side, :, :, part * 128:part * 128 + 128] = packed[:, which]
         turned = rope_f32[:, :rope].reshape(spots, owned, group, rope)
-        send_r[side] = jnp.concatenate(
+        send_first[side, :, :, kv:] = jnp.concatenate(
             [turned[:, which] for which in range(owned)], axis=-1
         ).astype(jnp.bfloat16)
 
@@ -217,11 +224,8 @@
         lax.fori_loop(1 - kind, spots, post, 0)
 
     def ship_queries(which, kind):
-        side = sides[kind]
-        if which == 0:
-            ship(send_r.at[side], recv_r, sr_sem.at[kind], rr_sem.at[kind], kind)
         ship(
-            send_q.at[side, which], recv_q.at[which],
+            sends[which].at[sides[kind]], recvs[which],
             sq_sem.at[which, kind], rq_sem.at[which, kind], kind,
         )
 
@@ -236,18 +240,20 @@
     across.wait_recv()
     queries(other)
     ship_queries(0, 1)
+    for which in range(1, owned):
+        for kind in range(2):
+            ship_queries(which, kind)
     keep = [
-        pltpu.make_async_copy(send_q.at[core, which, spot], recv_q.at[which, core, spot], own_sem.at[which])
+        pltpu.make_async_copy(sends[which].at[core, spot], recvs[which].at[core, spot], own_sem.at[which])
         for which in range(owned)
-    ] + [pltpu.make_async_copy(send_r.at[core, spot], recv_r.at[core, spot], own_sem.at[owned])]
+    ]
     for copy in keep:
         copy.start()
     for copy in keep:
         copy.wait()
 
     def turn_queries(kind):
-        settle(recv_r.at[sides[kind]], rr_sem.at[kind], kind)
-        turn = recv_r[sides[kind]].astype(jnp.float32)
+        turn = recv_first[sides[kind], :, :, kv:].astype(jnp.float32)
         width = turn.shape[2]
         flat = turn.reshape(spots * group, width)
         lane = lax.broadcasted_iota(jnp.int32, (1, width), 1)
@@ -260,15 +266,12 @@
         rotated = turn * cosine[None] + swapped * sine[None]
         turned_f32[kind] = rotated.reshape(spots * group, width)
 
-    for number, (which, kind) in enumerate(pieces):
+    for which, kind in pieces:
         side = sides[kind]
-        if number + 2 < len(pieces):
-            settle(send_q.at[side, which], sq_sem.at[which, kind], kind)
-            ship_queries(*pieces[number + 2])
+        settle(recvs[which].at[side], rq_sem.at[which, kind], kind)
         if which == 0:
             turn_queries(kind)
-        settle(recv_q.at[which, side], rq_sem.at[which, kind], kind)
-        query[:, :kv] = recv_q[which, side].reshape(spots * group, kv)
+        query[:, :kv] = recvs[which][side, :, :, :kv].reshape(spots * group, kv)
         query[:, kv:] = turned_f32[kind, :, which * rope:(which + 1) * rope].astype(jnp.bfloat16)
         if kind == 0:
             loads[which].wait()
@@ -308,11 +311,8 @@
     landed(gather.at[core, pl.ds(0, lines - 1), place], ga_sem)
     landed(gather.at[core, :, pl.ds(0, plane - 1)], gb_sem)
     across.wait_send()
-    for kind in range(2):
-        settle(send_r.at[sides[kind]], sr_sem.at[kind], kind)
-    for number, (which, kind) in enumerate(pieces):
-        if number + 2 >= len(pieces):
-            settle(send_q.at[sides[kind], which], sq_sem.at[which, kind], kind)
+    for which, kind in pieces:
+        settle(sends[which].at[sides[kind]], sq_sem.at[which, kind], kind)
         settle(send_o.at[which, sides[kind]], so_sem.at[which, kind], kind)
 
 
@@ -354,10 +354,10 @@
             pltpu.VMEM((kv // 128, rows * heads_here // cores, 128), f32),
             pltpu.VMEM((rows * heads_here // cores, owned * rope), f32),
             pltpu.VMEM((cores, spots * group, owned * rope), f32),
-            pltpu.VMEM((cores, owned, spots, group, kv), bf16),
-            pltpu.VMEM((cores, spots, group, owned * rope), bf16),
-            pltpu.VMEM((owned, cores, spots, group, kv), bf16),
-            pltpu.VMEM((cores, spots, group, owned * rope), bf16),
+            pltpu.VMEM((cores, spots, group, kv + owned * rope), bf16),
+            pltpu.VMEM((max(owned - 1, 1), cores, spots, group, kv), bf16),
+            pltpu.VMEM((cores, spots, group, kv + owned * rope), bf16),
+            pltpu.VMEM((max(owned - 1, 1), cores, spots, group, kv), bf16),
             pltpu.VMEM((spots * group, width), bf16),
             pltpu.VMEM((spots * group, ctx), f32),
             pltpu.VMEM((spots * group, min(128, chunk)), f32),
@@ -365,9 +365,8 @@
             pltpu.VMEM((spots * group, kv), f32),
             pltpu.VMEM((owned, cores, spots, group, kv), bf16),
             pltpu.VMEM((owned, cores, spots, group, kv), bf16),
-            dma((owned,)), dma, dma, dma, dma((owned + 1,)), dma, dma, dma, dma, dma, dma,
-            dma((owned, cores)), dma((cores,)), dma((owned, cores)),
-            dma((owned, cores)), dma((cores,)), dma((owned, cores)),
+            dma((owned,)), dma, dma, dma, dma((owned + 1,)), dma, dma, dma, dma((lines,)), dma, dma,
+            dma((owned, cores)), dma((owned, cores)), dma((owned, cores)), dma((owned, cores)),
         ],
         compiler_params=pltpu.CompilerParams(
             collective_id=0, has_side_effects=True, vmem_limit_bytes=56 << 20

time: 70.9 us -> 67.1 us (0.946)
  Pallas kernels: 68.8 us -> 65.1 us
    pallas_call x1, Pallas kernels: 68.8 us -> 65.1 us  [per_device(): pl.pallas_call(functools.partial(kernel, n, drafts, heads_here, nope, rop...]
where the time goes in v4:
time: 67.1 us; the launch traced here: 66.9 us
  Pallas kernels  65.1 us (97%)
  local copies, waits for them, and re-layouts  1.74 us (3%)
    pallas_call x1, Pallas kernels, per_device(): pl.pallas_call(functools.partial(kernel, n, drafts, heads_here, nope, rop...  65.1 us
    unnamed x1, local copies, waits for them, and re-layouts  1.74 us

profile of v4, /device:TPU:1, one launch (start us, length us, event | category | flops | bytes accessed | tf_op | source)
XLA Modules:
  0.0 66.9 jit_solution(14649954807949953488)
XLA Ops:
  0.0 65.1 %shard_map.73 = bf16[16,2,2,4,512]{4,3,2,1,0:T(4,128)(2,1)} custom-call(s32[2]{0:T(128)} %bitcast.10, s32[2]{0:T(128)} %bitcast.11, bf16[2,4,1536]{2,1,0:T(4,128)(2,1)} %bitcast.9, bf16[2,576,4096]{2,1,0:T(8,128)(2,1)} %bitcast.7, bf16[1536,768]{1,0:T(8,128)(2,1)} %wq_hbm, bf16[4,128,512]{2,1,0:T(8,128)(2,1)} %wk_hbm.1, bf16[4,512,128]{2,1,0:T(8,128)(2,1)} %wv_hbm.1), custom_call_target="tpu_custom_call" | custom-call | tf_op jit(solution)/shard_map/pallas_call | solution.py:341
  65.1 1.7 %copy.9 = bf16[1,64,4,512]{3,2,1,0:T(4,128)(2,1)} copy(bf16[1,64,4,512]{3,2,1,0:T(4,128)(2,1)} %bitcast.8) | data formatting | bytes 524288

commit v5 on v4

--- a/solution.py
+++ b/solution.py
@@ -40,7 +40,7 @@
     return jnp.cos(angle), sine
 
 
-def attend(which, length, query, cache, scores, peak_part, sum_part, acc, drafts, group, kv, coef, chunk):
+def attend(which, length, query, cache, flat, scores, peak_part, sum_part, acc, drafts, group, kv, coef, chunk):
     rows = query.shape[0]
     ctx = cache.shape[2]
     lanes = peak_part.shape[1]
@@ -74,9 +74,9 @@
         base = pl.multiple_of(step * chunk, chunk)
         part = jnp.exp2(scores[:, pl.ds(base, chunk)] * coef - peak)
         sum_part[...] += fold(part, jnp.add)
-        acc[...] += lax.dot_general(
-            part.astype(jnp.bfloat16), cache[which, :kv, pl.ds(base, chunk)],
-            (((1,), (1,)), ((), ())), preferred_element_type=jnp.float32,
+        acc[...] += jnp.dot(
+            part.astype(jnp.bfloat16), flat[which, pl.ds(base, chunk), :],
+            preferred_element_type=jnp.float32,
         )
         return carry
 
@@ -88,7 +88,7 @@
     n, drafts, heads_here, nope, rope, kv, vd, coef, chunk,
     length_ref, start_ref, latent_ref, cache_hbm, wq_hbm, wk_hbm, wv_hbm,
     out_ref,
-    cache, wq, wk, wv, gather, own_f32, q_full, wide_f32, rope_f32, turned_f32, send_first, send_q, recv_first, recv_q,
+    cache, flat, wq, wk, wv, gather, own_f32, q_full, wide_f32, rope_f32, turned_f32, send_first, send_q, recv_first, recv_q,
     query, scores, peak_part, sum_part, acc, send_o, recv_o,
     cache_sem, wq_sem, wk_sem, wv_sem, own_sem, ga_sem, gb_sem, gc_sem, ha_sem, hb_sem, hc_sem,
     sq_sem, so_sem, rq_sem, ro_sem,
@@ -164,6 +164,18 @@
         source = lax.rem(line + lines - t, lines)
         landed(gather.at[core, source, place], ha_sem.at[t])
         to_plane(source)
+    def flatten(which):
+        loads[which].wait()
+        size = min(512, chunk)
+
+        def turn(step, carry):
+            base = pl.multiple_of(step * size, size)
+            flat[which, pl.ds(base, size), :] = cache[which, :kv, pl.ds(base, size)].T
+            return carry
+
+        lax.fori_loop(0, cache.shape[2] // size, turn, 0)
+
+    flatten(0)
     landed(gather.at[core, :, pl.ds(0, plane - 1)], hb_sem)
     across = pltpu.make_async_remote_copy(
         src_ref=gather.at[core], dst_ref=gather.at[core], send_sem=gc_sem, recv_sem=hc_sem,
@@ -252,6 +264,9 @@
     for copy in keep:
         copy.wait()
 
+    for which in range(1, owned):
+        flatten(which)
+
     def turn_queries(kind):
         turn = recv_first[sides[kind], :, :, kv:].astype(jnp.float32)
         width = turn.shape[2]
@@ -273,10 +288,8 @@
             turn_queries(kind)
         query[:, :kv] = recvs[which][side, :, :, :kv].reshape(spots * group, kv)
         query[:, kv:] = turned_f32[kind, :, which * rope:(which + 1) * rope].astype(jnp.bfloat16)
-        if kind == 0:
-            loads[which].wait()
         latents = attend(
-            which, length_ref[which], query, cache, scores, peak_part, sum_part, acc,
+            which, length_ref[which], query, cache, flat, scores, peak_part, sum_part, acc,
             drafts, group, kv, coef, chunk,
         )
         send_o[which, side] = latents.astype(jnp.bfloat16).reshape(spots, group, kv)
@@ -345,6 +358,7 @@
         out_specs=vmem,
         scratch_shapes=[
             pltpu.VMEM((owned, width, ctx), bf16),
+            pltpu.VMEM((owned, ctx, kv), bf16),
             pltpu.VMEM(wq.shape, bf16),
             pltpu.VMEM(w_k_absorb.shape, bf16),
             pltpu.VMEM(value_up_weight.shape, bf16),

time: 67.1 us -> 67.2 us (level)
  no operation moved by 1% of the time
where the time goes in v5:
time: 67.2 us; the launch traced here: 67 us
  Pallas kernels  65.2 us (97%)
  local copies, waits for them, and re-layouts  1.74 us (3%)
    pallas_call x1, Pallas kernels, per_device(): pl.pallas_call(functools.partial(kernel, n, drafts, heads_here, nope, rop...  65.2 us
    unnamed x1, local copies, waits for them, and re-layouts  1.74 us

profile of v5, /device:TPU:1, one launch (start us, length us, event | category | flops | bytes accessed | tf_op | source)
XLA Modules:
  0.0 67.0 jit_solution(7353451922765130214)
XLA Ops:
  0.0 65.2 %shard_map.73 = bf16[16,2,2,4,512]{4,3,2,1,0:T(4,128)(2,1)} custom-call(s32[2]{0:T(128)} %bitcast.10, s32[2]{0:T(128)} %bitcast.11, bf16[2,4,1536]{2,1,0:T(4,128)(2,1)} %bitcast.9, bf16[2,576,4096]{2,1,0:T(8,128)(2,1)} %bitcast.7, bf16[1536,768]{1,0:T(8,128)(2,1)} %wq_hbm, bf16[4,128,512]{2,1,0:T(8,128)(2,1)} %wk_hbm.1, bf16[4,512,128]{2,1,0:T(8,128)(2,1)} %wv_hbm.1), custom_call_target="tpu_custom_call" | custom-call | tf_op jit(solution)/shard_map/pallas_call | solution.py:354
  65.2 1.7 %copy.9 = bf16[1,64,4,512]{3,2,1,0:T(4,128)(2,1)} copy(bf16[1,64,4,512]{3,2,1,0:T(4,128)(2,1)} %bitcast.8) | data formatting | bytes 524288

commit v6 on v5

--- a/solution.py
+++ b/solution.py
@@ -67,7 +67,7 @@
         peak_part[...] = jnp.maximum(peak_part[...], fold(part, jnp.maximum))
         return carry
 
-    lax.fori_loop(0, ctx // chunk, score, 0)
+    lax.fori_loop(0, ctx // chunk, score, 0, unroll=True)
     peak = jnp.max(peak_part[...], axis=1, keepdims=True) * coef
 
     def weigh(step, carry):
@@ -80,7 +80,7 @@
         )
         return carry
 
-    lax.fori_loop(0, ctx // chunk, weigh, 0)
+    lax.fori_loop(0, ctx // chunk, weigh, 0, unroll=True)
     return acc[...] * (1.0 / jnp.sum(sum_part[...], axis=1, keepdims=True))
 
 

time: 67.2 us -> 67.2 us (level)
  no operation moved by 1% of the time
where the time goes in v6:
time: 67.2 us; the launch traced here: 67 us
  Pallas kernels  65.2 us (97%)
  local copies, waits for them, and re-layouts  1.74 us (3%)
    pallas_call x1, Pallas kernels, per_device(): pl.pallas_call(functools.partial(kernel, n, drafts, heads_here, nope, rop...  65.2 us
    unnamed x1, local copies, waits for them, and re-layouts  1.74 us

profile of v6, /device:TPU:1, one launch (start us, length us, event | category | flops | bytes accessed | tf_op | source)
XLA Modules:
  0.0 67.0 jit_solution(8138369963971058207)
XLA Ops:
  0.0 65.2 %shard_map.73 = bf16[16,2,2,4,512]{4,3,2,1,0:T(4,128)(2,1)} custom-call(s32[2]{0:T(128)} %bitcast.10, s32[2]{0:T(128)} %bitcast.11, bf16[2,4,1536]{2,1,0:T(4,128)(2,1)} %bitcast.9, bf16[2,576,4096]{2,1,0:T(8,128)(2,1)} %bitcast.7, bf16[1536,768]{1,0:T(8,128)(2,1)} %wq_hbm, bf16[4,128,512]{2,1,0:T(8,128)(2,1)} %wk_hbm.1, bf16[4,512,128]{2,1,0:T(8,128)(2,1)} %wv_hbm.1), custom_call_target="tpu_custom_call" | custom-call | tf_op jit(solution)/shard_map/pallas_call | solution.py:354
  65.2 1.7 %copy.9 = bf16[1,64,4,512]{3,2,1,0:T(4,128)(2,1)} copy(bf16[1,64,4,512]{3,2,1,0:T(4,128)(2,1)} %bitcast.8) | data formatting | bytes 524288
